TPU v7x, 256 devices: a whole 4x4x8 slice. The times are simulated.
256 devices in a mesh: gx: 16 (over x, z_hi, core), gy: 4 (over y), gz: 4 (over z_lo).
Axes of the slice: x: 4, y: 4, z: 8 (z_hi: 2, z_lo: 4; z = z_hi * 4 + z_lo), core: 2. Of those that a mesh axis runs over, the one named last changes fastest.
Arguments:
- fine_state: bfloat16 [262144, 512], P(('gx', 'gy', 'gz')), may hold values from -6 to 6
- fine_nbrs: int32 [262144, 6], P(('gx', 'gy', 'gz')), may hold values from 0 to 1792, as said below
- send_rows: int32 [256, 6, 128], P(('gx', 'gy', 'gz')), may hold values from 0 to 1023
- ghost_counts: int32 [256, 6], P(('gx', 'gy', 'gz')), may hold values from 32 to 128, as said below
- fine_parent: int32 [262144], P(('gx', 'gy', 'gz')), may hold values from 0 to 127, as said below
- medium_state: bfloat16 [32768, 512], P(('gx', 'gy', 'gz')), may hold values from -6 to 6
- medium_parent: int32 [32768], P(('gx', 'gy', 'gz')), may hold values from 0 to 15, as said below
- coarse_state: bfloat16 [4096, 512], P(('gx', 'gy', 'gz')), may hold values from -6 to 6
- coarse_nbrs: int32 [4096, 64], P(('gx', 'gy', 'gz')), may hold values from 0 to 4095, as said below
- fine_edge_in: bfloat16 [1024, 512], replicated, may hold values from -0.1875 to 0.1875
- fine_edge_bias: float32 [512], replicated, may hold values from -3 to 3
- fine_edge_out: bfloat16 [512, 512], replicated, may hold values from -0.25 to 0.25
- fine_edge_gain: float32 [512], replicated, may hold values from 0.1 to 1.9
- fine_node_in: bfloat16 [1024, 512], replicated, may hold values from -0.1875 to 0.1875
- fine_node_bias: float32 [512], replicated, may hold values from -3 to 3
- fine_node_out: bfloat16 [512, 512], replicated, may hold values from -0.25 to 0.25
- fine_node_gain: float32 [512], replicated, may hold values from 0.1 to 1.9
- coarse_edge_in: bfloat16 [1024, 512], replicated, may hold values from -0.1875 to 0.1875
- coarse_edge_bias: float32 [512], replicated, may hold values from -3 to 3
- coarse_edge_out: bfloat16 [512, 512], replicated, may hold values from -0.25 to 0.25
- coarse_edge_gain: float32 [512], replicated, may hold values from 0.1 to 1.9
- coarse_node_in: bfloat16 [1024, 512], replicated, may hold values from -0.1875 to 0.1875
- coarse_node_bias: float32 [512], replicated, may hold values from -3 to 3
- coarse_node_out: bfloat16 [512, 512], replicated, may hold values from -0.25 to 0.25
- coarse_node_gain: float32 [512], replicated, may hold values from 0.1 to 1.9
Outputs:
- fine_out: bfloat16 [262144, 512], P(('gx', 'gy', 'gz'))
- medium_out: bfloat16 [32768, 512], P(('gx', 'gy', 'gz'))
- coarse_out: bfloat16 [4096, 512], P(('gx', 'gy', 'gz'))
Inputs may be any that keep to these rules, and one draw needn't show every extreme that they name: `fine_nbrs`: row i of device p lists node i's neighbours as rows of table_p: 0 to 1023 own nodes, then 6 ghost blocks of 128 rows in the order of ghosts; a ghost row is named only if the sending neighbour exists and the row lies below that neighbour's count for the face it sends. The value 1024 + 6 * 128 marks an empty slot; empty slots follow the used ones, and at least 4 slots of every row are used. `ghost_counts`: entry f of device p counts the used rows of the block that p sends from face f; on every device one face is full. `send_rows`: local fine rows of the sending device; rows at or past the face's count are not used. `fine_parent`: A local medium index of the same device; every medium node has at least one child. `medium_parent`: A local coarse index of the same device; every coarse node has at least one child. `coarse_nbrs`: global coarse rows anywhere on the mesh.
All inputs are finite; a program needn't handle non-finite values.
Results may differ from a plain program's by a relative error of at most 0.0075.
Values may be sent and summed in bfloat16 or wider, within the bound.
No kernel may reach another device: no remote copies, remote signals or barrier semaphores. Data moves between devices by JAX's collectives and lax.ppermute only.
A program may use at most 128 MiB of HBM per device.

v0:
```python
import jax
import jax.numpy as jnp
from jax import lax
from jax.sharding import Mesh
from jax.sharding import PartitionSpec as P

GX = ("gx_0", "gx_1", "gx_2")
GX_GY_GZ = ("gx_0", "gx_1", "gx_2", "gy", "gz")


def extended(block, sides, width):
    for axis, dim in sides:
        count = lax.axis_size(axis)
        forward = [(i, i + 1) for i in range(count - 1)]
        backward = [(target, source) for source, target in forward]
        low = lax.ppermute(
            lax.slice_in_dim(block, block.shape[dim] - width, None, axis=dim), axis, forward
        )
        high = lax.ppermute(lax.slice_in_dim(block, 0, width, axis=dim), axis, backward)
        block = jnp.concatenate([low, block, high], axis=dim)
    return block


def edges_of(length, count):
    lap = length // count
    if lap >= 8:
        lap -= lap % 8
    return [lap * k for k in range(1, count)]


def stacked_from(shard, axes, order):
    parts = shard[None]
    for k in order:
        parts = lax.all_gather(parts, axes[k], axis=0, tiled=True)
    block = [lax.axis_size(axes[k]) for k in reversed(order)]
    parts = parts.reshape(*block, *shard.shape)
    turned = sorted(range(len(order)), key=lambda place: order[len(order) - 1 - place])
    return parts.transpose(*turned, *range(len(order), parts.ndim)).reshape(-1, *shard.shape)


def joined_along(parts, dim):
    parts = jnp.moveaxis(parts, 0, dim)
    shape = parts.shape
    return parts.reshape(*shape[:dim], shape[dim] * shape[dim + 1], *shape[dim + 2 :])


def gather_at_once(shard, axes, dim):
    numbers = list(range(len(axes)))[::-1]
    widest = shard.shape.index(max(shard.shape[:-1] or shard.shape))
    edges = [0, *edges_of(shard.shape[widest], len(axes)), shard.shape[widest]]
    finished = []
    for k, (start, end) in enumerate(zip(edges, edges[1:])):
        if end > start:
            share = lax.slice_in_dim(shard, start, end, axis=widest)
            finished.append(stacked_from(share, axes, numbers[k:] + numbers[:k]))
    return joined_along(jnp.concatenate(finished, axis=widest + 1), dim)


def layer_norm(values):
    center = values - jnp.mean(values, axis=-1, keepdims=True)
    spread = jnp.mean(center * center, axis=-1, keepdims=True)
    return center * lax.rsqrt(spread + 1e-05)


def edge_messages(sender_rows, receiver, biases, out_weight, gains, slot_count):
    features = receiver.shape[1]
    combined = (
        sender_rows.astype(jnp.float32).reshape(-1, slot_count, features)
        + receiver[:, None, :]
        + biases
    )
    hidden = jax.nn.relu(combined).astype(jnp.bfloat16).reshape(-1, features)
    return layer_norm(jnp.dot(hidden, out_weight, preferred_element_type=jnp.float32)) * gains


def node_update(current, incoming, in_weight, biases, out_weight, gains):
    features = current.shape[1]
    combined = jnp.dot(current, in_weight[:features], preferred_element_type=jnp.float32)
    combined = (
        combined
        + jnp.dot(incoming, in_weight[features:], preferred_element_type=jnp.float32)
        + biases
    )
    hidden = jax.nn.relu(combined).astype(jnp.bfloat16)
    return layer_norm(jnp.dot(hidden, out_weight, preferred_element_type=jnp.float32)) * gains


def trade_states(outgoing):
    traded_first = extended(outgoing[0:2], ((GX, 0),), 1)
    traded_second = extended(outgoing[2:4], (("gy", 0),), 1)
    traded_third = extended(outgoing[4:6], (("gz", 0),), 1)
    return jnp.concatenate(
        [
            traded_first[0],
            traded_first[3],
            traded_second[0],
            traded_second[3],
            traded_third[0],
            traded_third[3],
        ],
        axis=0,
    )


def local(
    fine_state,
    fine_nbrs,
    send_rows,
    ghost_counts,
    fine_parent,
    medium_state,
    medium_parent,
    coarse_state,
    coarse_nbrs,
    fine_edge_in,
    fine_edge_bias,
    fine_edge_out,
    fine_edge_gain,
    fine_node_in,
    fine_node_bias,
    fine_node_out,
    fine_node_gain,
    coarse_edge_in,
    coarse_edge_bias,
    coarse_edge_out,
    coarse_edge_gain,
    coarse_node_in,
    coarse_node_bias,
    coarse_node_out,
    coarse_node_gain,
):
    own_rows, features = fine_state.shape
    slot_count = fine_nbrs.shape[1]
    face_rows = send_rows.shape[2]
    sender_weight = fine_edge_in[:features]
    receiver = jnp.dot(fine_state, fine_edge_in[features:], preferred_element_type=jnp.float32)
    in_count = lax.broadcasted_iota(jnp.int32, (6, face_rows), 1) < ghost_counts.reshape(6, 1)
    picked = jnp.take(fine_state, send_rows.reshape(-1), axis=0).reshape(6, face_rows, features)
    outgoing = jnp.where(in_count[:, :, None], picked, jnp.zeros_like(picked))
    ghosts = trade_states(outgoing)
    lookup = jnp.concatenate([fine_state, ghosts, jnp.zeros((1, features), jnp.bfloat16)], axis=0)
    sender = jnp.dot(lookup, sender_weight, preferred_element_type=jnp.float32).astype(jnp.bfloat16)
    messages = edge_messages(
        jnp.take(sender, fine_nbrs.reshape(-1), axis=0),
        receiver,
        fine_edge_bias,
        fine_edge_out,
        fine_edge_gain,
        slot_count,
    )
    live_slots = (fine_nbrs < own_rows + 6 * face_rows).astype(jnp.float32)
    incoming = jnp.sum(
        messages.reshape(own_rows, slot_count, features) * live_slots[:, :, None], axis=1
    ).astype(jnp.bfloat16)
    fine_new = fine_state.astype(jnp.float32) + node_update(
        fine_state, incoming, fine_node_in, fine_node_bias, fine_node_out, fine_node_gain
    )
    medium_rows = medium_state.shape[0]
    coarse_rows = coarse_state.shape[0]
    fine_member = fine_parent[None, :] == lax.broadcasted_iota(
        jnp.int32, (medium_rows, own_rows), 0
    )
    child_sum = jnp.dot(
        fine_member.astype(jnp.bfloat16), fine_state, preferred_element_type=jnp.float32
    )
    child_count = jnp.sum(fine_member.astype(jnp.float32), axis=1, keepdims=True)
    medium_pool = medium_state.astype(jnp.float32) + child_sum / child_count
    medium_member = (
        medium_parent[None, :] == lax.broadcasted_iota(jnp.int32, (coarse_rows, medium_rows), 0)
    ).astype(jnp.float32)
    coarse_sum = jnp.dot(medium_member, medium_pool, precision=lax.Precision.HIGHEST)
    coarse_pool = (
        coarse_state.astype(jnp.float32)
        + coarse_sum / jnp.sum(medium_member, axis=1, keepdims=True)
    ).astype(jnp.bfloat16)
    coarse_flat = coarse_nbrs.reshape(-1)
    link_count = coarse_nbrs.shape[1]
    coarse_sender_weight = coarse_edge_in[:features]
    all_rows = gather_at_once(coarse_pool, GX_GY_GZ, 0)
    coarse_sender = jnp.dot(
        jnp.take(all_rows, coarse_flat, axis=0),
        coarse_sender_weight,
        preferred_element_type=jnp.float32,
    ).astype(jnp.bfloat16)
    coarse_receiver = jnp.dot(
        coarse_pool, coarse_edge_in[features:], preferred_element_type=jnp.float32
    )
    coarse_msgs = edge_messages(
        coarse_sender,
        coarse_receiver,
        coarse_edge_bias,
        coarse_edge_out,
        coarse_edge_gain,
        link_count,
    )
    coarse_incoming = jnp.sum(
        coarse_msgs.reshape(coarse_rows, link_count, features), axis=1
    ).astype(jnp.bfloat16)
    coarse_delta = node_update(
        coarse_pool,
        coarse_incoming,
        coarse_node_in,
        coarse_node_bias,
        coarse_node_out,
        coarse_node_gain,
    )
    coarse_final = (coarse_pool.astype(jnp.float32) + coarse_delta).astype(jnp.bfloat16)
    medium_delta = jnp.take(coarse_delta, medium_parent, axis=0)
    medium_final = (medium_pool + medium_delta).astype(jnp.bfloat16)
    fine_final = (fine_new + jnp.take(medium_delta, fine_parent, axis=0)).astype(jnp.bfloat16)
    return (fine_final, medium_final, coarse_final)


def solution(mesh):
    torus = Mesh(
        mesh.devices.reshape(4, 2, 2, mesh.shape["gy"], mesh.shape["gz"]),
        ("gx_0", "gx_1", "gx_2", "gy", "gz"),
    )
    placed = (
        P(GX_GY_GZ, None),
        P(GX_GY_GZ, None),
        P(GX_GY_GZ, None, None),
        P(GX_GY_GZ, None),
        P(GX_GY_GZ),
        P(GX_GY_GZ, None),
        P(GX_GY_GZ),
        P(GX_GY_GZ, None),
        P(GX_GY_GZ, None),
        P(),
        P(),
        P(),
        P(),
        P(),
        P(),
        P(),
        P(),
        P(),
        P(),
        P(),
        P(),
        P(),
        P(),
        P(),
        P(),
    )
    return jax.shard_map(
        local,
        mesh=torus,
        in_specs=placed,
        out_specs=(P(GX_GY_GZ, None), P(GX_GY_GZ, None), P(GX_GY_GZ, None)),
        check_vma=False,
    )
```

profile of v0, /device:TPU:40, one launch (start us, length us, event | category | flops | bytes accessed | tf_op | source)
XLA Modules:
  0.0 503.5 jit_solution(556025854398983436)
XLA Ops:
  30.2 19.0 %all-gather.9 = bf16[4,4,512]{2,1,0:T(4,128)(2,1)S(1)} all-gather(bf16[1,4,512]{2,1,0:T(4,128)(2,1)S(1)} %slice_bitcast_fusion), channel_id=6, replica_groups=mesh['gx_0'=4,'gx_1'=2,'gx_2'=2,'gy'=4,'gz'=4] {'gx_0'}, dimensions={0}, use_global_device_ids=true | all-gather | bytes 20480 | tf_op jit(solution)/shard_map/all_gather | solution.py:34
  49.2 11.5 %all_gather.96 = bf16[16,4,512]{2,1,0:T(4,128)(2,1)S(1)} all-gather(bf16[4,4,512]{2,1,0:T(4,128)(2,1)S(1)} %all-gather.9), channel_id=1, replica_groups=mesh['gx_0'=4,'gx_1'=2,'gx_2'=2,'gy'=4,'gz'=4] {'gz'}, dimensions={0}, use_global_device_ids=true | all-gather | bytes 81920 | tf_op jit(solution)/shard_map/all_gather | solution.py:34
  60.7 12.5 %all_gather.97 = bf16[64,4,512]{2,1,0:T(4,128)(2,1)S(1)} all-gather(bf16[16,4,512]{2,1,0:T(4,128)(2,1)S(1)} %all_gather.96), channel_id=1, replica_groups=mesh['gx_0'=4,'gx_1'=2,'gx_2'=2,'gy'=4,'gz'=4] {'gy'}, dimensions={0}, use_global_device_ids=true | all-gather | bytes 327680 | tf_op jit(solution)/shard_map/all_gather | solution.py:34
  90.7 9.7 %add.203 = f32[1024,6,512]{2,1,0:T(8,128)} broadcast(f32[1024,512]{1,0:T(8,128)} %fusion.33), dimensions={0,2} | broadcast | bytes 14680064 | tf_op jit(solution)/shard_map/add | solution.py:68
  100.4 15.7 %add.204 = f32[6144,512]{1,0:T(8,128)} reshape(f32[1024,6,512]{2,1,0:T(8,128)} %add.203) | data formatting | bytes 25165824 | tf_op jit(solution)/shard_map/add | solution.py:68
  127.5 11.9 %all_gather.91 = bf16[8,3,512]{2,1,0:T(4,128)(2,1)S(1)} all-gather(bf16[2,3,512]{2,1,0:T(4,128)(2,1)S(1)} %all-gather.8), channel_id=1, replica_groups=mesh['gx_0'=4,'gx_1'=2,'gx_2'=2,'gy'=4,'gz'=4] {'gx_0'}, dimensions={0}, use_global_device_ids=true | all-gather | bytes 30720 | tf_op jit(solution)/shard_map/all_gather | solution.py:34
  139.4 13.3 %all_gather.92 = bf16[32,3,512]{2,0,1:T(8,128)(2,1)S(1)} all-gather(bf16[8,3,512]{2,0,1:T(8,128)(2,1)S(1)} %copy.72), channel_id=1, replica_groups=mesh['gx_0'=4,'gx_1'=2,'gx_2'=2,'gy'=4,'gz'=4] {'gz'}, dimensions={0}, use_global_device_ids=true | all-gather | bytes 122880 | tf_op jit(solution)/shard_map/all_gather | solution.py:34
  152.7 12.5 %all_gather.93 = bf16[128,3,512]{2,0,1:T(8,128)(2,1)S(1)} all-gather(bf16[32,3,512]{2,0,1:T(8,128)(2,1)S(1)} %all_gather.92), channel_id=1, replica_groups=mesh['gx_0'=4,'gx_1'=2,'gx_2'=2,'gy'=4,'gz'=4] {'gy'}, dimensions={0}, use_global_device_ids=true | all-gather | bytes 491520 | tf_op jit(solution)/shard_map/all_gather | solution.py:34
  179.8 11.9 %all_gather.87 = bf16[16,3,512]{2,1,0:T(4,128)(2,1)S(1)} all-gather(bf16[4,3,512]{2,1,0:T(4,128)(2,1)S(1)} %all_gather.86), channel_id=1, replica_groups=mesh['gx_0'=4,'gx_1'=2,'gx_2'=2,'gy'=4,'gz'=4] {'gx_0'}, dimensions={0}, use_global_device_ids=true | all-gather | bytes 61440 | tf_op jit(solution)/shard_map/all_gather | solution.py:34
  191.6 13.7 %all_gather.88 = bf16[64,3,512]{2,0,1:T(8,128)(2,1)S(1)} all-gather(bf16[16,3,512]{2,0,1:T(8,128)(2,1)S(1)} %copy.70), channel_id=1, replica_groups=mesh['gx_0'=4,'gx_1'=2,'gx_2'=2,'gy'=4,'gz'=4] {'gz'}, dimensions={0}, use_global_device_ids=true | all-gather | bytes 245760 | tf_op jit(solution)/shard_map/all_gather | solution.py:34
  205.3 13.3 %all_gather.89 = bf16[256,3,512]{2,0,1:T(8,128)(2,1)S(1)} all-gather(bf16[64,3,512]{2,0,1:T(8,128)(2,1)S(1)} %all_gather.88), channel_id=1, replica_groups=mesh['gx_0'=4,'gx_1'=2,'gx_2'=2,'gy'=4,'gz'=4] {'gy'}, dimensions={0}, use_global_device_ids=true | all-gather | bytes 983040 | tf_op jit(solution)/shard_map/all_gather | solution.py:34
  220.6 12.0 %all-gather.6 = bf16[4,3,512]{2,1,0:T(4,128)(2,1)S(1)} all-gather(bf16[1,3,512]{2,1,0:T(4,128)(2,1)} %get-tuple-element.27), channel_id=3, replica_groups=mesh['gx_0'=4,'gx_1'=2,'gx_2'=2,'gy'=4,'gz'=4] {'gy'}, dimensions={0}, use_global_device_ids=true | all-gather | bytes 15360 | tf_op jit(solution)/shard_map/all_gather | solution.py:34
  234.4 8.5 %all_gather.82 = bf16[16,3,512]{2,0,1:T(8,128)(2,1)S(1)} all-gather(bf16[8,3,512]{2,0,1:T(8,128)(2,1)S(1)} %copy.68), channel_id=1, replica_groups=mesh['gx_0'=4,'gx_1'=2,'gx_2'=2,'gy'=4,'gz'=4] {'gx_1'}, dimensions={0}, use_global_device_ids=true | all-gather | bytes 73728 | tf_op jit(solution)/shard_map/all_gather | solution.py:34
  242.9 12.2 %all_gather.83 = bf16[64,3,512]{2,0,1:T(8,128)(2,1)S(1)} all-gather(bf16[16,3,512]{2,0,1:T(8,128)(2,1)S(1)} %all_gather.82), channel_id=1, replica_groups=mesh['gx_0'=4,'gx_1'=2,'gx_2'=2,'gy'=4,'gz'=4] {'gx_0'}, dimensions={0}, use_global_device_ids=true | all-gather | bytes 245760 | tf_op jit(solution)/shard_map/all_gather | solution.py:34
  255.1 17.5 %all_gather.84 = bf16[256,3,512]{2,0,1:T(8,128)(2,1)S(1)} all-gather(bf16[64,3,512]{2,0,1:T(8,128)(2,1)S(1)} %all_gather.83), channel_id=1, replica_groups=mesh['gx_0'=4,'gx_1'=2,'gx_2'=2,'gy'=4,'gz'=4] {'gz'}, dimensions={0}, use_global_device_ids=true | all-gather | bytes 983040 | tf_op jit(solution)/shard_map/all_gather | solution.py:34
  274.4 13.7 %all-gather.5 = bf16[4,3,512]{2,1,0:T(4,128)(2,1)S(1)} all-gather(bf16[1,3,512]{2,1,0:T(4,128)(2,1)} %get-tuple-element.28), channel_id=2, replica_groups=mesh['gx_0'=4,'gx_1'=2,'gx_2'=2,'gy'=4,'gz'=4] {'gz'}, dimensions={0}, use_global_device_ids=true | all-gather | bytes 15360 | tf_op jit(solution)/shard_map/all_gather | solution.py:34
  288.1 11.8 %all_gather.76 = bf16[16,3,512]{2,1,0:T(4,128)(2,1)S(1)} all-gather(bf16[4,3,512]{2,1,0:T(4,128)(2,1)S(1)} %all-gather.5), channel_id=1, replica_groups=mesh['gx_0'=4,'gx_1'=2,'gx_2'=2,'gy'=4,'gz'=4] {'gy'}, dimensions={0}, use_global_device_ids=true | all-gather | bytes 61440 | tf_op jit(solution)/shard_map/all_gather | solution.py:34
  301.9 11.7 %all_gather.78 = bf16[64,3,512]{2,0,1:T(8,128)(2,1)S(1)} all-gather(bf16[32,3,512]{2,0,1:T(8,128)(2,1)S(1)} %all_gather.77), channel_id=1, replica_groups=mesh['gx_0'=4,'gx_1'=2,'gx_2'=2,'gy'=4,'gz'=4] {'gx_1'}, dimensions={0}, use_global_device_ids=true | all-gather | bytes 294912 | tf_op jit(solution)/shard_map/all_gather | solution.py:34
  313.5 14.2 %all_gather.79 = bf16[256,3,512]{2,0,1:T(8,128)(2,1)S(1)} all-gather(bf16[64,3,512]{2,0,1:T(8,128)(2,1)S(1)} %all_gather.78), channel_id=1, replica_groups=mesh['gx_0'=4,'gx_1'=2,'gx_2'=2,'gy'=4,'gz'=4] {'gx_0'}, dimensions={0}, use_global_device_ids=true | all-gather | bytes 983040 | tf_op jit(solution)/shard_map/all_gather | solution.py:34
  338.1 25.7 %gather_fusion.1 = bf16[6144,512]{1,0:T(8,128)(2,1)} fusion(bf16[1793,512]{1,0:T(8,128)(2,1)S(1)} %convolution_convert_fusion, s32[6144]{0:T(1024)S(1)} %copy-done.12), kind=kCustom, calls=%fused_computation.1 | custom fusion | bytes 12607488 | tf_op jit(solution)/shard_map/jit(_take)/gather | solution.py:144
  363.8 9.5 %fusion.56 = (f32[6144]{0:T(1024)S(1)}, f32[6144,512]{1,0:T(8,128)S(1)}) fusion(bf16[512,512]{1,0:T(8,128)(2,1)S(1)} %copy-done, f32[6144,512]{1,0:T(8,128)} %add.204, f32[512]{0:T(512)S(1)} %copy-done.23, bf16[6144,512]{1,0:T(8,128)(2,1)} %gather_fusion.1, pred[6144]{0:T(1024)(128)(4,1)S(1)} %copy-done.15), kind=kOutput, calls=%fused_computation.121 | convolution fusion | flops 3243239424 | bytes 32014336 | tf_op jit(solution)/shard_map/dot_general | solution.py:73
  381.0 15.1 %reshape.275 = f32[1024,6,512]{2,1,0:T(8,128)} reshape(f32[6144,512]{1,0:T(8,128)} %multiply_multiply_fusion) | data formatting | bytes 25165824 | tf_op jit(solution)/shard_map/reshape | solution.py:153
  396.1 10.4 %multiply_reduce_fusion = bf16[1024,512]{1,0:T(8,128)(2,1)} fusion(f32[1024,6,512]{2,1,0:T(8,128)} %reshape.275, f32[1024,6]{1,0:T(8,128)S(1)} %copy-done.3), kind=kLoop, calls=%fused_computation.5 | loop fusion | flops 5767168 | bytes 13656064 | tf_op jit(solution)/shard_map/reduce_sum | solution.py:152
  413.0 54.2 %concatenate.7 = bf16[256,16,512]{2,1,0:T(8,128)(2,1)} concatenate(bf16[256,3,512]{2,1,0:T(4,128)(2,1)} %copy.75, bf16[256,3,512]{2,1,0:T(4,128)(2,1)} %bitcast.81, bf16[256,3,512]{2,1,0:T(4,128)(2,1)} %bitcast.80, bf16[256,3,512]{2,1,0:T(4,128)(2,1)} %bitcast.79, bf16[256,4,512]{2,1,0:T(4,128)(2,1)} %bitcast.82), dimensions={1} | concatenate | bytes 8388608 | tf_op jit(solution)/shard_map/concatenate | solution.py:56
  (175 shorter events, 127.6 us)
Async XLA Ops:
  7.2 356.6 %copy-start = (bf16[512,512]{1,0:T(8,128)(2,1)S(1)}, bf16[512,512]{1,0:T(8,128)(2,1)}, u32[]{:S(2)}) copy-start(bf16[512,512]{1,0:T(8,128)(2,1)} %param.36) | copy-start | bytes 1572868
  7.2 403.1 %all-gather.12.cloned.1.call-start = ((), (), s32[]{:S(2)}) async-start(), calls=%async_computation | async-start | bytes 1572864 | tf_op jit(solution)/shard_map/all_gather | solution.py:34
  14.2 15.2 %copy-start.16 = (s32[1024]{0:T(1024)S(1)}, s32[1024]{0:T(1024)}, u32[]{:S(2)}) copy-start(s32[1024]{0:T(1024)} %param.29) | copy-start | bytes 12292
  14.2 15.3 %copy-start.31 = (s32[128]{0:T(128)S(1)}, s32[128]{0:T(128)}, u32[]{:S(2)}) copy-start(s32[128]{0:T(128)} %param.31) | copy-start | bytes 1540
  14.2 15.4 %copy-start.2 = (bf16[1024,512]{1,0:T(8,128)(2,1)S(1)}, bf16[1024,512]{1,0:T(8,128)(2,1)}, u32[]{:S(2)}) copy-start(bf16[1024,512]{1,0:T(8,128)(2,1)} %param.25) | copy-start | bytes 3145732
  14.2 15.4 %copy-start.34 = (bf16[128,512]{1,0:T(8,128)(2,1)S(1)}, bf16[128,512]{1,0:T(8,128)(2,1)}, u32[]{:S(2)}) copy-start(bf16[128,512]{1,0:T(8,128)(2,1)} %param.30) | copy-start | bytes 393220
  14.5 15.5 %copy-start.20 = (bf16[16,512]{1,0:T(8,128)(2,1)S(1)}, bf16[16,512]{1,0:T(8,128)(2,1)}, u32[]{:S(2)}) copy-start(bf16[16,512]{1,0:T(8,128)(2,1)} %param.32) | copy-start | bytes 49156
  15.4 314.5 %collective-permute-start = (bf16[1,128,512]{2,1,0:T(8,128)(2,1)}, bf16[1,128,512]{2,1,0:T(8,128)(2,1)}, u32[]{:S(2)}, u32[]{:S(2)}) collective-permute-start(bf16[1,128,512]{2,1,0:T(8,128)(2,1)} %get-tuple-element.24), channel_id=1, source_target_pairs={{0,16},{16,32},{32,48},{48,64},{64,80},{80,96},{96,112},{112,128},... | collective-permute-start | bytes 393224 | tf_op jit(solution)/shard_map/ppermute | solution.py:16
  17.8 315.1 %collective-permute-start.1 = (bf16[1,128,512]{2,1,0:T(8,128)(2,1)}, bf16[1,128,512]{2,1,0:T(8,128)(2,1)}, u32[]{:S(2)}, u32[]{:S(2)}) collective-permute-start(bf16[1,128,512]{2,1,0:T(8,128)(2,1)} %get-tuple-element.23), channel_id=1, source_target_pairs={{16,0},{32,16},{48,32},{64,48},{80,64},{96,80},{112,96},{128,112},... | collective-permute-start | bytes 393224 | tf_op jit(solution)/shard_map/ppermute | solution.py:19
  19.0 314.7 %collective-permute-start.2 = (bf16[1,128,512]{2,1,0:T(8,128)(2,1)}, bf16[1,128,512]{2,1,0:T(8,128)(2,1)}, u32[]{:S(2)}, u32[]{:S(2)}) collective-permute-start(bf16[1,128,512]{2,1,0:T(8,128)(2,1)} %get-tuple-element.22), channel_id=1, source_target_pairs={{0,4},{4,8},{8,12},{1,5},{5,9},{9,13},{2,6},{6,10},{10,14},{3,7},{... | collective-permute-start | bytes 393224 | tf_op jit(solution)/shard_map/ppermute | solution.py:16
  22.5 312.2 %collective-permute-start.3 = (bf16[1,128,512]{2,1,0:T(8,128)(2,1)}, bf16[1,128,512]{2,1,0:T(8,128)(2,1)}, u32[]{:S(2)}, u32[]{:S(2)}) collective-permute-start(bf16[1,128,512]{2,1,0:T(8,128)(2,1)} %get-tuple-element.21), channel_id=1, source_target_pairs={{4,0},{8,4},{12,8},{5,1},{9,5},{13,9},{6,2},{10,6},{14,10},{7,3},{... | collective-permute-start | bytes 393224 | tf_op jit(solution)/shard_map/ppermute | solution.py:19
  25.5 310.1 %collective-permute-start.4 = (bf16[1,128,512]{2,1,0:T(8,128)(2,1)}, bf16[1,128,512]{2,1,0:T(8,128)(2,1)}, u32[]{:S(2)}, u32[]{:S(2)}) collective-permute-start(bf16[1,128,512]{2,1,0:T(8,128)(2,1)} %get-tuple-element.20), channel_id=1, source_target_pairs={{0,1},{1,2},{2,3},{4,5},{5,6},{6,7},{8,9},{9,10},{10,11},{12,13},{... | collective-permute-start | bytes 393224 | tf_op jit(solution)/shard_map/ppermute | solution.py:16
  75.5 13.2 %copy-start.8 = (bf16[1024,512]{1,0:T(8,128)(2,1)S(1)}, bf16[1024,512]{1,0:T(8,128)(2,1)}, u32[]{:S(2)}) copy-start(bf16[1024,512]{1,0:T(8,128)(2,1)} %param.34) | copy-start | bytes 3145732
  100.4 15.7 %copy-start.11 = (f32[1024,6]{0,1:T(8,128)S(1)}, f32[1024,6]{0,1:T(8,128)}, u32[]{:S(2)}) copy-start(f32[1024,6]{0,1:T(8,128)} %compare_convert_fusion) | copy-start | bytes 73732
  100.4 16.7 %copy-start.10 = (bf16[1024,512]{1,0:T(8,128)(2,1)S(1)}, bf16[1024,512]{1,0:T(8,128)(2,1)}, u32[]{:S(2)}) copy-start(bf16[1024,512]{1,0:T(8,128)(2,1)} %param.38) | copy-start | bytes 3145732
  274.4 55.0 %copy-start.5 = (bf16[1024,512]{1,0:T(8,128)(2,1)S(1)}, bf16[1024,512]{1,0:T(8,128)(2,1)}, u32[]{:S(2)}) copy-start(bf16[1024,512]{1,0:T(8,128)(2,1)} %param.42) | copy-start | bytes 3145732
  274.4 55.1 %copy-start.21 = (s32[1024]{0:T(1024)S(1)}, s32[1024]{0:T(1024)}, u32[]{:S(2)}) copy-start(s32[1024]{0:T(1024)} %reshape.276) | copy-start | bytes 12292
  274.4 55.1 %copy-start.4 = (bf16[1024,512]{1,0:T(8,128)(2,1)S(1)}, bf16[1024,512]{1,0:T(8,128)(2,1)}, u32[]{:S(2)}) copy-start(bf16[1024,512]{1,0:T(8,128)(2,1)} %param.46) | copy-start | bytes 3145732
  301.9 27.9 %copy-start.33 = (s32[128]{0:T(128)S(1)}, s32[128]{0:T(128)}, u32[]{:S(2)}) copy-start(s32[128]{0:T(128)} %compare_select_fusion.7) | copy-start | bytes 1540
  329.9 7.0 %collective-permute-start.5 = (bf16[1,128,512]{2,1,0:T(8,128)(2,1)S(1)}, bf16[1,128,512]{2,1,0:T(8,128)(2,1)S(1)}, u32[]{:S(2)}, u32[]{:S(2)}) collective-permute-start(bf16[1,128,512]{2,1,0:T(8,128)(2,1)S(1)} %get-tuple-element.19), channel_id=1, source_target_pairs={{1,0},{2,1},{3,2},{5,4},{6,5},{7,6},{9,8},{10,9},{11,10},{13,12},{... | collective-permute-start | bytes 393224 | tf_op jit(solution)/shard_map/ppermute | solution.py:19
  338.0 25.8 %copy-start.15 = (pred[6144]{0:T(1024)(128)(4,1)S(1)}, pred[6144]{0:T(1024)(128)(4,1)}, u32[]{:S(2)}) copy-start(pred[6144]{0:T(1024)(128)(4,1)} %compare_and_fusion) | copy-start | bytes 18436
  338.1 25.7 %copy-start.23 = (f32[512]{0:T(512)S(1)}, f32[512]{0:T(512)}, u32[]{:S(2)}) copy-start(f32[512]{0:T(512)} %param.35) | copy-start | bytes 6148
  381.0 15.1 %copy-start.3 = (f32[1024,6]{1,0:T(8,128)S(1)}, f32[1024,6]{1,0:T(8,128)}, u32[]{:S(2)}) copy-start(f32[1024,6]{1,0:T(8,128)} %copy.66) | copy-start | bytes 73732
  413.0 54.2 %copy-start.19 = (s32[1024]{0:T(1024)S(1)}, s32[1024]{0:T(1024)}, u32[]{:S(2)}) copy-start(s32[1024]{0:T(1024)} %get-tuple-element.38) | copy-start | bytes 12292
  (19 other events, 85.8 us)
Sparse Core Ops, SparseCore 0:
  75.6 42.7 all-gather.11
where the time goes:
time: 509 us; the launch traced here: 503 us
  blocking collectives  248 us (49%)
  local copies, waits for them, and re-layouts  167 us (33%)
  other arithmetic  33.9 us (7%)
  matrix products  23.5 us (5%)
  starting transfers between devices  16.1 us (3%)
  between operations  14.6 us (3%)
    all_gather x24, blocking collectives, stacked_from(): parts = lax.all_gather(parts, axes[k], axis=0, tiled=True)  248 us
    concatenate x1, local copies, waits for them, and re-layouts, gather_at_once(): return joined_along(jnp.concatenate(finished, axis=widest + 1), dim)  54.2 us
    gather x1, local copies, waits for them, and re-layouts, local(): jnp.take(sender, fine_nbrs.reshape(-1), axis=0)  25.7 us
    add x2, local copies, waits for them, and re-layouts, edge_messages(): sender_rows.astype(jnp.float32).reshape(-1, slot_count, features)  25.4 us
    reshape x1, local copies, waits for them, and re-layouts, local(): messages.reshape(own_rows, slot_count, features) * live_slots[:, :, None]  15.1 us
    reduce_sum x1, other arithmetic, local(): jnp.sum(messages.reshape(own_rows, slot_count, features) * live_slots[:,...  10.4 us
    dot_general x2, matrix products, edge_messages(): jnp.dot(hidden, out_weight, preferred_element_type=jnp.float32)  10.3 us
    unnamed x84, local copies, waits for them, and re-layouts  10.2 us
  transfers between devices with their start and end apart: 7, of which 1 were waited for; matrix products, arithmetic and copies ran while one was open for 26% of the time, Pallas kernels for 0%

commit v1 on v0

--- a/solution.py
+++ b/solution.py
@@ -31,7 +31,9 @@
 def stacked_from(shard, axes, order):
     parts = shard[None]
     for k in order:
-        parts = lax.all_gather(parts, axes[k], axis=0, tiled=True)
+        parts = jnp.concatenate(
+            lax.all_to_all(jnp.stack([parts] * lax.axis_size(axes[k])), axes[k], 0, 0), axis=0
+        )
     block = [lax.axis_size(axes[k]) for k in reversed(order)]
     parts = parts.reshape(*block, *shard.shape)
     turned = sorted(range(len(order)), key=lambda place: order[len(order) - 1 - place])

time: 509 us -> 470 us (0.923)
  blocking collectives: 248 us -> 18.2 us
  starting transfers between devices: 16.1 us -> 110 us
  waiting for transfers between devices: 0.35 us -> 76.3 us
  local copies, waits for them, and re-layouts: 167 us -> 183 us
  between operations: 14.6 us -> 1.45 us
  other arithmetic: 33.9 us -> 46.3 us
    all_gather x24 -> x0, blocking collectives: 248 us -> none  [stacked_from(): parts = lax.all_gather(parts, axes[k], axis=0, tiled=True)]
    all_to_all x0 -> x21, starting transfers between devices: none -> 93.6 us  [stacked_from(): lax.all_to_all(jnp.stack([parts] * lax.axis_size(axes[k])), axes[k], 0, 0)]
    all_to_all x0 -> x21, waiting for transfers between devices: none -> 76.3 us  [stacked_from(): lax.all_to_all(jnp.stack([parts] * lax.axis_size(axes[k])), axes[k], 0, 0)]
    all_to_all x0 -> x4, blocking collectives: none -> 18.2 us  [stacked_from(): lax.all_to_all(jnp.stack([parts] * lax.axis_size(axes[k])), axes[k], 0, 0)]
    another operation x0 -> x26, local copies, waits for them, and re-layouts: none -> 15.7 us  [the longest x25 12.9 us: stacked_from(): jnp.stack([parts] * lax.axis_size(axes[k]))]
    mul x1, other arithmetic: 5.2 us -> 10.7 us  [edge_messages(): layer_norm(jnp.dot(hidden, out_weight, preferred_element_type=jnp.float32))]
    unnamed x84 -> x110, local copies, waits for them, and re-layouts: 10.2 us -> 14 us
  transfers between devices with their start and end apart: 7 -> 27, of which waited for: 1 -> 17; matrix products, arithmetic and copies ran while one was open for 26% -> 34% of each run, Pallas kernels for 0% -> 0%
where the time goes in v1:
time: 470 us; the launch traced here: 462 us
  local copies, waits for them, and re-layouts  183 us (39%)
  starting transfers between devices  110 us (23%)
  waiting for transfers between devices  76.3 us (16%)
  other arithmetic  46.3 us (10%)
  matrix products  26.8 us (6%)
  blocking collectives  18.2 us (4%)
    all_to_all x21, starting transfers between devices, stacked_from(): lax.all_to_all(jnp.stack([parts] * lax.axis_size(axes[k])), axes[k], 0, 0)  93.6 us
    all_to_all x21, waiting for transfers between devices, stacked_from(): lax.all_to_all(jnp.stack([parts] * lax.axis_size(axes[k])), axes[k], 0, 0)  76.3 us
    concatenate x1, local copies, waits for them, and re-layouts, gather_at_once(): return joined_along(jnp.concatenate(finished, axis=widest + 1), dim)  54.1 us
    gather x1, local copies, waits for them, and re-layouts, local(): jnp.take(sender, fine_nbrs.reshape(-1), axis=0)  25.4 us
    add x2, local copies, waits for them, and re-layouts, edge_messages(): sender_rows.astype(jnp.float32).reshape(-1, slot_count, features)  25.3 us
    all_to_all x4, blocking collectives, stacked_from(): lax.all_to_all(jnp.stack([parts] * lax.axis_size(axes[k])), axes[k], 0, 0)  18.2 us
    reshape x1, local copies, waits for them, and re-layouts, local(): messages.reshape(own_rows, slot_count, features) * live_slots[:, :, None]  15 us
    unnamed x110, local copies, waits for them, and re-layouts  14 us
  transfers between devices with their start and end apart: 27, of which 17 were waited for; matrix products, arithmetic and copies ran while one was open for 34% of the time, Pallas kernels for 0%

profile of v1, /device:TPU:40, one launch (start us, length us, event | category | flops | bytes accessed | tf_op | source)
XLA Modules:
  0.0 461.6 jit_solution(12762121511236501162)
XLA Ops:
  25.0 6.1 %all-to-all-start.10 = ((bf16[2,1,3,512]{3,2,1,0:T(4,128)(2,1)}), bf16[2,1,3,512]{3,2,1,0:T(4,128)(2,1)S(1)}, u32[]{:S(2)}, u32[]{:S(2)}) async-start(bf16[2,1,3,512]{3,2,1,0:T(4,128)(2,1)} %pad_maximum_fusion.8), calls=%async_computation.10 | async-start | bytes 16384 | tf_op jit(solution)/shard_map/all_to_all | solution.py:35
  49.5 9.6 %all-to-all-start.15 = ((bf16[2,1,3,512]{3,2,1,0:T(4,128)(2,1)}), bf16[2,1,3,512]{3,2,1,0:T(4,128)(2,1)S(1)}, u32[]{:S(2)}, u32[]{:S(2)}) async-start(bf16[2,1,3,512]{3,2,1,0:T(4,128)(2,1)} %pad_maximum_fusion.9), calls=%async_computation.15 | async-start | bytes 16384 | tf_op jit(solution)/shard_map/all_to_all | solution.py:35
  59.2 7.7 %all-to-all-done.15 = bf16[2,1,3,512]{3,2,1,0:T(4,128)(2,1)S(1)} async-done(((bf16[2,1,3,512]{3,2,1,0:T(4,128)(2,1)}), bf16[2,1,3,512]{3,2,1,0:T(4,128)(2,1)S(1)}, u32[]{:S(2)}, u32[]{:S(2)}) %all-to-all-start.15) | async-done | bytes 6176 | tf_op jit(solution)/shard_map/all_to_all | solution.py:35
  84.8 7.2 %all-to-all-done.11 = bf16[2,2,3,512]{3,1,2,0:T(2,128)(2,1)S(1)} async-done(((bf16[2,2,3,512]{3,1,2,0:T(2,128)(2,1)}), bf16[2,2,3,512]{3,1,2,0:T(2,128)(2,1)S(1)}, u32[]{:S(2)}, u32[]{:S(2)}) %all-to-all-start.11) | async-done | bytes 12320 | tf_op jit(solution)/shard_map/all_to_all | solution.py:35
  110.1 9.7 %add.203 = f32[1024,6,512]{2,1,0:T(8,128)} broadcast(f32[1024,512]{1,0:T(8,128)} %fusion.33), dimensions={0,2} | broadcast | bytes 14680064 | tf_op jit(solution)/shard_map/add | solution.py:70
  119.7 15.7 %add.204 = f32[6144,512]{1,0:T(8,128)} reshape(f32[1024,6,512]{2,1,0:T(8,128)} %add.203) | data formatting | bytes 25165824 | tf_op jit(solution)/shard_map/add | solution.py:70
  142.0 5.5 %all-to-all-done.12 = bf16[4,4,3,512]{3,1,2,0:T(4,128)(2,1)S(1)} async-done(((bf16[4,4,3,512]{3,1,2,0:T(4,128)(2,1)}), bf16[4,4,3,512]{3,1,2,0:T(4,128)(2,1)S(1)}, u32[]{:S(2)}, u32[]{:S(2)}) %all-to-all-start.12) | async-done | bytes 49184 | tf_op jit(solution)/shard_map/all_to_all | solution.py:35
  164.5 7.4 %all-to-all-done.7 = bf16[2,8,3,512]{3,1,2,0:T(8,128)(2,1)S(1)} async-done(((bf16[2,8,3,512]{3,1,2,0:T(8,128)(2,1)}), bf16[2,8,3,512]{3,1,2,0:T(8,128)(2,1)S(1)}, u32[]{:S(2)}, u32[]{:S(2)}) %all-to-all-start.7) | async-done | bytes 49184 | tf_op jit(solution)/shard_map/all_to_all | solution.py:35
  196.7 5.4 %all-to-all-done.8 = bf16[4,16,3,512]{3,1,2,0:T(8,128)(2,1)S(1)} async-done(((bf16[4,16,3,512]{3,1,2,0:T(8,128)(2,1)}), bf16[4,16,3,512]{3,1,2,0:T(8,128)(2,1)S(1)}, u32[]{:S(2)}, u32[]{:S(2)}) %all-to-all-start.8) | async-done | bytes 196640 | tf_op jit(solution)/shard_map/all_to_all | solution.py:35
  218.2 7.9 %all-to-all-done.3 = bf16[2,32,3,512]{3,1,2,0:T(8,128)(2,1)S(1)} async-done(((bf16[2,32,3,512]{3,1,2,0:T(8,128)(2,1)}), bf16[2,32,3,512]{3,1,2,0:T(8,128)(2,1)S(1)}, u32[]{:S(2)}, u32[]{:S(2)}) %all-to-all-start.3) | async-done | bytes 196640 | tf_op jit(solution)/shard_map/all_to_all | solution.py:35
  226.1 4.9 %all_to_all.127 = bf16[2,64,4,512]{3,2,1,0:T(4,128)(2,1)} all-to-all(bf16[2,64,4,512]{3,2,1,0:T(4,128)(2,1)S(1)} %pad_maximum_fusion.2), channel_id=1, replica_groups=mesh['gx_0'=4,'gx_1'=2,'gx_2'=2,'gy'=4,'gz'=4] {'gx_2'}, dimensions={0} | all-to-all | bytes 1048576 | tf_op jit(solution)/shard_map/all_to_all | solution.py:35
  231.7 4.9 %all-to-all-start.18 = ((bf16[4,32,3,512]{3,1,2,0:T(8,128)(2,1)}), bf16[4,32,3,512]{3,1,2,0:T(8,128)(2,1)S(1)}, u32[]{:S(2)}, u32[]{:S(2)}) async-start(bf16[4,32,3,512]{3,1,2,0:T(8,128)(2,1)} %stack.93), calls=%async_computation.18 | async-start | bytes 786432 | tf_op jit(solution)/shard_map/all_to_all | solution.py:35
  238.8 5.1 %all-to-all-done.18 = bf16[4,32,3,512]{3,1,2,0:T(8,128)(2,1)S(1)} async-done(((bf16[4,32,3,512]{3,1,2,0:T(8,128)(2,1)}), bf16[4,32,3,512]{3,1,2,0:T(8,128)(2,1)S(1)}, u32[]{:S(2)}, u32[]{:S(2)}) %all-to-all-start.18) | async-done | bytes 393248 | tf_op jit(solution)/shard_map/all_to_all | solution.py:35
  250.6 25.4 %gather_fusion.1 = bf16[6144,512]{1,0:T(8,128)(2,1)} fusion(bf16[1793,512]{1,0:T(8,128)(2,1)S(1)} %convolution_convert_fusion, s32[6144]{0:T(1024)S(1)} %copy-done.25), kind=kCustom, calls=%fused_computation.1 | custom fusion | bytes 12607488 | tf_op jit(solution)/shard_map/jit(_take)/gather | solution.py:146
  276.2 5.2 %all_to_all.128 = bf16[2,128,3,512]{3,1,2,0:T(8,128)(2,1)} all-to-all(bf16[2,128,3,512]{3,1,2,0:T(8,128)(2,1)S(1)} %pad_maximum_fusion.1), channel_id=1, replica_groups=mesh['gx_0'=4,'gx_1'=2,'gx_2'=2,'gy'=4,'gz'=4] {'gx_2'}, dimensions={0} | all-to-all | bytes 1572864 | tf_op jit(solution)/shard_map/all_to_all | solution.py:35
  286.0 11.2 %fusion.56 = (f32[6144]{0:T(1024)S(1)}, f32[6144,512]{1,0:T(8,128)}) fusion(bf16[512,512]{1,0:T(8,128)(2,1)S(1)} %copy-done, f32[6144,512]{1,0:T(8,128)} %add.204, f32[512]{0:T(512)S(1)} %copy-done.37, bf16[6144,512]{1,0:T(8,128)(2,1)} %gather_fusion.1, pred[6144]{0:T(1024)(128)(4,1)S(1)} %compare_and_fusion), kind=kOutput, calls=%fused_computation.130 | convolution fusion | flops 3243239424 | bytes 32014336 | tf_op jit(solution)/shard_map/dot_general | solution.py:75
  299.6 4.9 %all-to-all-start.14 = ((bf16[4,64,3,512]{3,1,2,0:T(8,128)(2,1)}), bf16[4,64,3,512]{3,1,2,0:T(8,128)(2,1)S(1)}, u32[]{:S(2)}, u32[]{:S(2)}) async-start(bf16[4,64,3,512]{3,1,2,0:T(8,128)(2,1)} %stack.89), calls=%async_computation.14 | async-start | bytes 1572864 | tf_op jit(solution)/shard_map/all_to_all | solution.py:35
  304.5 6.0 %multiply_reduce_fusion.1 = f32[6144]{0:T(1024)S(1)} fusion(f32[6144,512]{1,0:T(8,128)} %get-tuple-element.43, f32[6144]{0:T(1024)S(1)} %broadcast_multiply_fusion), kind=kLoop, calls=%fused_computation.7 | loop fusion | flops 9431040 | bytes 12632064 | tf_op jit(solution)/shard_map/reduce_sum | solution.py:63
  319.6 10.7 %multiply_multiply_fusion = f32[6144,512]{1,0:T(8,128)} fusion(f32[6144,512]{1,0:T(8,128)} %get-tuple-element.43, f32[512]{0:T(512)S(1)} %copy-done.41, f32[6144]{0:T(1024)S(1)} %add_rsqrt_fusion, f32[6144]{0:T(1024)S(1)} %broadcast_multiply_fusion), kind=kLoop, calls=%fused_computation.6 | loop fusion | flops 9437184 | bytes 25217024 | tf_op jit(solution)/shard_map/mul | solution.py:75
  330.3 15.0 %reshape.293 = f32[1024,6,512]{2,1,0:T(8,128)} reshape(f32[6144,512]{1,0:T(8,128)} %multiply_multiply_fusion) | data formatting | bytes 25165824 | tf_op jit(solution)/shard_map/reshape | solution.py:155
  352.3 10.4 %multiply_reduce_fusion = bf16[1024,512]{1,0:T(8,128)(2,1)} fusion(f32[1024,6,512]{2,1,0:T(8,128)} %reshape.293, f32[1024,6]{1,0:T(8,128)S(1)} %copy-done.8), kind=kLoop, calls=%fused_computation.5 | loop fusion | flops 5767168 | bytes 13656064 | tf_op jit(solution)/shard_map/reduce_sum | solution.py:154
  377.9 54.1 %concatenate.7 = bf16[256,16,512]{2,1,0:T(8,128)(2,1)} concatenate(bf16[256,3,512]{2,1,0:T(4,128)(2,1)} %bitcast.100, bf16[256,3,512]{2,1,0:T(4,128)(2,1)} %bitcast.102, bf16[256,3,512]{2,1,0:T(4,128)(2,1)} %bitcast.101, bf16[256,3,512]{2,1,0:T(4,128)(2,1)} %bitcast.99, bf16[256,4,512]{2,1,0:T(4,128)(2,1)} %bitcast.103), dimensions={1} | concatenate | bytes 8388608 | tf_op jit(solution)/shard_map/concatenate | solution.py:58
  432.1 7.9 %gather_fusion.2 = bf16[1024,512]{1,0:T(8,128)(2,1)} fusion(bf16[4096,512]{1,0:T(8,128)(2,1)} %bitcast.98, s32[1024]{0:T(1024)S(1)} %copy-done.33), kind=kCustom, calls=%fused_computation.2 | custom fusion | bytes 2101248 | tf_op jit(solution)/shard_map/jit(_take)/gather | solution.py:183
  448.1 4.9 %gather_fusion.4 = f32[1024,512]{1,0:T(8,128)} fusion(f32[128,512]{1,0:T(8,128)S(1)} %get-tuple-element.27, s32[1024]{0:T(1024)S(1)} %copy-done.34), kind=kCustom, calls=%fused_computation.4 | custom fusion | bytes 4198400 | tf_op jit(solution)/shard_map/jit(_take)/gather | solution.py:212
  (263 shorter events, 207.5 us)
Async XLA Ops:
  8.8 168.2 %collective-permute-start = (bf16[1,128,512]{2,1,0:T(8,128)(2,1)}, bf16[1,128,512]{2,1,0:T(8,128)(2,1)}, u32[]{:S(2)}, u32[]{:S(2)}) collective-permute-start(bf16[1,128,512]{2,1,0:T(8,128)(2,1)} %get-tuple-element.33), channel_id=1, source_target_pairs={{0,16},{16,32},{32,48},{48,64},{64,80},{80,96},{96,112},{112,128},... | collective-permute-start | bytes 393224 | tf_op jit(solution)/shard_map/ppermute | solution.py:16
  11.3 175.5 %collective-permute-start.1 = (bf16[1,128,512]{2,1,0:T(8,128)(2,1)}, bf16[1,128,512]{2,1,0:T(8,128)(2,1)}, u32[]{:S(2)}, u32[]{:S(2)}) collective-permute-start(bf16[1,128,512]{2,1,0:T(8,128)(2,1)} %get-tuple-element.32), channel_id=1, source_target_pairs={{16,0},{32,16},{48,32},{64,48},{80,64},{96,80},{112,96},{128,112},... | collective-permute-start | bytes 393224 | tf_op jit(solution)/shard_map/ppermute | solution.py:19
  12.6 183.2 %collective-permute-start.2 = (bf16[1,128,512]{2,1,0:T(8,128)(2,1)}, bf16[1,128,512]{2,1,0:T(8,128)(2,1)}, u32[]{:S(2)}, u32[]{:S(2)}) collective-permute-start(bf16[1,128,512]{2,1,0:T(8,128)(2,1)} %get-tuple-element.31), channel_id=1, source_target_pairs={{0,4},{4,8},{8,12},{1,5},{5,9},{9,13},{2,6},{6,10},{10,14},{3,7},{... | collective-permute-start | bytes 393224 | tf_op jit(solution)/shard_map/ppermute | solution.py:16
  16.0 191.6 %collective-permute-start.3 = (bf16[1,128,512]{2,1,0:T(8,128)(2,1)}, bf16[1,128,512]{2,1,0:T(8,128)(2,1)}, u32[]{:S(2)}, u32[]{:S(2)}) collective-permute-start(bf16[1,128,512]{2,1,0:T(8,128)(2,1)} %get-tuple-element.30), channel_id=1, source_target_pairs={{4,0},{8,4},{12,8},{5,1},{9,5},{13,9},{6,2},{10,6},{14,10},{7,3},{... | collective-permute-start | bytes 393224 | tf_op jit(solution)/shard_map/ppermute | solution.py:19
  19.0 197.3 %collective-permute-start.4 = (bf16[1,128,512]{2,1,0:T(8,128)(2,1)}, bf16[1,128,512]{2,1,0:T(8,128)(2,1)}, u32[]{:S(2)}, u32[]{:S(2)}) collective-permute-start(bf16[1,128,512]{2,1,0:T(8,128)(2,1)} %get-tuple-element.29), channel_id=1, source_target_pairs={{0,1},{1,2},{2,3},{4,5},{5,6},{6,7},{8,9},{9,10},{10,11},{12,13},{... | collective-permute-start | bytes 393224 | tf_op jit(solution)/shard_map/ppermute | solution.py:16
  25.0 15.2 %all-to-all-start.10 = ((bf16[2,1,3,512]{3,2,1,0:T(4,128)(2,1)}), bf16[2,1,3,512]{3,2,1,0:T(4,128)(2,1)S(1)}, u32[]{:S(2)}, u32[]{:S(2)}) async-start(bf16[2,1,3,512]{3,2,1,0:T(4,128)(2,1)} %pad_maximum_fusion.8), calls=%async_computation.10 | async-start | bytes 16384 | tf_op jit(solution)/shard_map/all_to_all | solution.py:35
  49.5 17.3 %all-to-all-start.15 = ((bf16[2,1,3,512]{3,2,1,0:T(4,128)(2,1)}), bf16[2,1,3,512]{3,2,1,0:T(4,128)(2,1)S(1)}, u32[]{:S(2)}, u32[]{:S(2)}) async-start(bf16[2,1,3,512]{3,2,1,0:T(4,128)(2,1)} %pad_maximum_fusion.9), calls=%async_computation.15 | async-start | bytes 16384 | tf_op jit(solution)/shard_map/all_to_all | solution.py:35
  71.9 9.1 %all-to-all-start = ((bf16[4,1,3,512]{3,2,1,0:T(4,128)(2,1)}), bf16[4,1,3,512]{3,2,1,0:T(4,128)(2,1)S(1)}, u32[]{:S(2)}, u32[]{:S(2)}) async-start(bf16[4,1,3,512]{3,2,1,0:T(4,128)(2,1)} %stack.75), calls=%async_computation | async-start | bytes 32768 | tf_op jit(solution)/shard_map/all_to_all | solution.py:35
  81.0 11.0 %all-to-all-start.11 = ((bf16[2,2,3,512]{3,1,2,0:T(2,128)(2,1)}), bf16[2,2,3,512]{3,1,2,0:T(2,128)(2,1)S(1)}, u32[]{:S(2)}, u32[]{:S(2)}) async-start(bf16[2,2,3,512]{3,1,2,0:T(2,128)(2,1)} %copy.148), calls=%async_computation.11 | async-start | bytes 24576 | tf_op jit(solution)/shard_map/all_to_all | solution.py:35
  102.7 33.9 %all-to-all-start.16 = ((bf16[4,2,3,512]{3,1,2,0:T(2,128)(2,1)}), bf16[4,2,3,512]{3,1,2,0:T(2,128)(2,1)}, u32[]{:S(2)}, u32[]{:S(2)}) async-start(bf16[4,2,3,512]{3,1,2,0:T(2,128)(2,1)} %stack.91), calls=%async_computation.16 | async-start | bytes 49152 | tf_op jit(solution)/shard_map/all_to_all | solution.py:35
  137.2 10.3 %all-to-all-start.12 = ((bf16[4,4,3,512]{3,1,2,0:T(4,128)(2,1)}), bf16[4,4,3,512]{3,1,2,0:T(4,128)(2,1)S(1)}, u32[]{:S(2)}, u32[]{:S(2)}) async-start(bf16[4,4,3,512]{3,1,2,0:T(4,128)(2,1)} %stack.87), calls=%async_computation.12 | async-start | bytes 98304 | tf_op jit(solution)/shard_map/all_to_all | solution.py:35
  160.5 11.4 %all-to-all-start.7 = ((bf16[2,8,3,512]{3,1,2,0:T(8,128)(2,1)}), bf16[2,8,3,512]{3,1,2,0:T(8,128)(2,1)S(1)}, u32[]{:S(2)}, u32[]{:S(2)}) async-start(bf16[2,8,3,512]{3,1,2,0:T(8,128)(2,1)} %pad_maximum_fusion.5), calls=%async_computation.7 | async-start | bytes 98304 | tf_op jit(solution)/shard_map/all_to_all | solution.py:35
  172.6 9.5 %all-to-all-start.21 = ((bf16[4,4,4,512]{3,2,1,0:T(4,128)(2,1)}), bf16[4,4,4,512]{3,2,1,0:T(4,128)(2,1)S(1)}, u32[]{:S(2)}, u32[]{:S(2)}) async-start(bf16[4,4,4,512]{3,2,1,0:T(4,128)(2,1)} %stack.96), calls=%async_computation.21 | async-start | bytes 131072 | tf_op jit(solution)/shard_map/all_to_all | solution.py:35
  177.0 59.6 %collective-permute-start.5 = (bf16[1,128,512]{2,1,0:T(8,128)(2,1)}, bf16[1,128,512]{2,1,0:T(8,128)(2,1)}, u32[]{:S(2)}, u32[]{:S(2)}) collective-permute-start(bf16[1,128,512]{2,1,0:T(8,128)(2,1)} %get-tuple-element.28), channel_id=1, source_target_pairs={{1,0},{2,1},{3,2},{5,4},{6,5},{7,6},{9,8},{10,9},{11,10},{13,12},{... | collective-permute-start | bytes 393224 | tf_op jit(solution)/shard_map/ppermute | solution.py:19
  182.7 8.9 %all-to-all-start.17 = ((bf16[4,8,3,512]{3,1,2,0:T(8,128)(2,1)}), bf16[4,8,3,512]{3,1,2,0:T(8,128)(2,1)S(1)}, u32[]{:S(2)}, u32[]{:S(2)}) async-start(bf16[4,8,3,512]{3,1,2,0:T(8,128)(2,1)} %stack.92), calls=%async_computation.17 | async-start | bytes 196608 | tf_op jit(solution)/shard_map/all_to_all | solution.py:35
  192.4 9.7 %all-to-all-start.8 = ((bf16[4,16,3,512]{3,1,2,0:T(8,128)(2,1)}), bf16[4,16,3,512]{3,1,2,0:T(8,128)(2,1)S(1)}, u32[]{:S(2)}, u32[]{:S(2)}) async-start(bf16[4,16,3,512]{3,1,2,0:T(8,128)(2,1)} %stack.83), calls=%async_computation.8 | async-start | bytes 393216 | tf_op jit(solution)/shard_map/all_to_all | solution.py:35
  202.8 10.1 %all-to-all-start.22 = ((bf16[4,16,4,512]{3,2,1,0:T(4,128)(2,1)}), bf16[4,16,4,512]{3,2,1,0:T(4,128)(2,1)S(1)}, u32[]{:S(2)}, u32[]{:S(2)}) async-start(bf16[4,16,4,512]{3,2,1,0:T(4,128)(2,1)} %stack.97), calls=%async_computation.22 | async-start | bytes 524288 | tf_op jit(solution)/shard_map/all_to_all | solution.py:35
  212.9 13.2 %all-to-all-start.3 = ((bf16[2,32,3,512]{3,1,2,0:T(8,128)(2,1)}), bf16[2,32,3,512]{3,1,2,0:T(8,128)(2,1)S(1)}, u32[]{:S(2)}, u32[]{:S(2)}) async-start(bf16[2,32,3,512]{3,1,2,0:T(8,128)(2,1)} %pad_maximum_fusion.3), calls=%async_computation.3 | async-start | bytes 393216 | tf_op jit(solution)/shard_map/all_to_all | solution.py:35
  231.7 12.1 %all-to-all-start.18 = ((bf16[4,32,3,512]{3,1,2,0:T(8,128)(2,1)}), bf16[4,32,3,512]{3,1,2,0:T(8,128)(2,1)S(1)}, u32[]{:S(2)}, u32[]{:S(2)}) async-start(bf16[4,32,3,512]{3,1,2,0:T(8,128)(2,1)} %stack.93), calls=%async_computation.18 | async-start | bytes 786432 | tf_op jit(solution)/shard_map/all_to_all | solution.py:35
  244.5 31.7 %all-to-all-start.13 = ((bf16[4,16,3,512]{3,1,2,0:T(8,128)(2,1)}), bf16[4,16,3,512]{3,1,2,0:T(8,128)(2,1)S(1)}, u32[]{:S(2)}, u32[]{:S(2)}) async-start(bf16[4,16,3,512]{3,1,2,0:T(8,128)(2,1)} %stack.88), calls=%async_computation.13 | async-start | bytes 393216 | tf_op jit(solution)/shard_map/all_to_all | solution.py:35
  282.3 16.3 %all-to-all-start.4 = ((bf16[4,64,3,512]{3,1,2,0:T(8,128)(2,1)}), bf16[4,64,3,512]{3,1,2,0:T(8,128)(2,1)S(1)}, u32[]{:S(2)}, u32[]{:S(2)}) async-start(bf16[4,64,3,512]{3,1,2,0:T(8,128)(2,1)} %stack.79), calls=%async_computation.4 | async-start | bytes 1572864 | tf_op jit(solution)/shard_map/all_to_all | solution.py:35
  299.6 15.5 %all-to-all-start.14 = ((bf16[4,64,3,512]{3,1,2,0:T(8,128)(2,1)}), bf16[4,64,3,512]{3,1,2,0:T(8,128)(2,1)S(1)}, u32[]{:S(2)}, u32[]{:S(2)}) async-start(bf16[4,64,3,512]{3,1,2,0:T(8,128)(2,1)} %stack.89), calls=%async_computation.14 | async-start | bytes 1572864 | tf_op jit(solution)/shard_map/all_to_all | solution.py:35
  316.0 31.0 %all-to-all-start.24 = ((bf16[2,128,4,512]{3,2,1,0:T(4,128)(2,1)}), bf16[2,128,4,512]{3,2,1,0:T(4,128)(2,1)S(1)}, u32[]{:S(2)}, u32[]{:S(2)}) async-start(bf16[2,128,4,512]{3,2,1,0:T(4,128)(2,1)} %pad_maximum_fusion), calls=%async_computation.24 | async-start | bytes 2097152 | tf_op jit(solution)/shard_map/all_to_all | solution.py:35
  348.1 27.0 %all-to-all-start.9 = ((bf16[4,64,3,512]{3,1,2,0:T(8,128)(2,1)}), bf16[4,64,3,512]{3,1,2,0:T(8,128)(2,1)}, u32[]{:S(2)}, u32[]{:S(2)}) async-start(bf16[4,64,3,512]{3,1,2,0:T(8,128)(2,1)} %stack.84), calls=%async_computation.9 | async-start | bytes 1572864 | tf_op jit(solution)/shard_map/all_to_all | solution.py:35
  (53 other events, 777.3 us)
